TPU v7x, 512 devices: a whole 4x8x8 slice. The times are simulated.
512 devices in a mesh: dp: 64 (over z_hi, y, core), tensor: 8 (over x, z_lo).
Axes of the slice: x: 4, y: 8, z: 8 (z_hi: 4, z_lo: 2; z = z_hi * 2 + z_lo), core: 2. Of those that a mesh axis runs over, the one named last changes fastest.
Arguments:
- teacher: bfloat16 [16384, 3072], P('dp', 'tensor'), may hold values from -6 to 6
- projector: bfloat16 [3072, 2048], P('tensor', 'dp'), may hold values from -0.109375 to 0.109375
- residual: bfloat16 [16384, 2048], P(('dp', 'tensor')), may hold values from -6 to 6
- gate_pre: bfloat16 [16384, 8192], P('dp', 'tensor'), may hold values from -6 to 6
- up_pre: bfloat16 [16384, 8192], P('dp', 'tensor'), may hold values from -6 to 6
- down_weight: bfloat16 [8192, 2048], P('tensor', 'dp'), may hold values from -0.0625 to 0.0625
Outputs:
- projector_grad: float32 [3072, 2048], P('tensor', 'dp')
- grad_residual: bfloat16 [16384, 2048], P(('dp', 'tensor'))
- grad_gate: bfloat16 [16384, 8192], P('dp', 'tensor')
- grad_up: bfloat16 [16384, 8192], P('dp', 'tensor')
All inputs are finite; a program needn't handle non-finite values.
Results may differ from a plain program's by a relative error of at most 0.015.
Values may be sent and summed in bfloat16 or wider, within the bound.
A program may use at most 64 MiB of HBM per device.

v0:
```python
import math
import jax
import jax.numpy as jnp
from jax import lax
from jax.sharding import PartitionSpec as P


def per_device(teacher, projector, residual, gate_pre, up_pre, down_weight):
    group_rows = teacher.shape[0]
    ways = lax.axis_size("tensor")
    share = group_rows // ways
    token_total = group_rows * lax.axis_size("dp")
    gate = gate_pre.astype(jnp.float32)
    upper = up_pre.astype(jnp.float32)
    sig = jax.nn.sigmoid(gate)
    hidden = (gate * sig * upper).astype(jnp.bfloat16)
    projected = jnp.dot(
        teacher,
        lax.all_gather(projector, "dp", axis=1, tiled=True),
        preferred_element_type=jnp.float32,
    )
    down_whole = lax.all_gather(down_weight, "dp", axis=1, tiled=True)
    mlp_term = jnp.dot(hidden, down_whole, preferred_element_type=jnp.float32)
    parts = mlp_term - projected
    stacked = parts.astype(jnp.bfloat16).reshape(ways, share, parts.shape[1])
    received = lax.all_to_all(stacked, "tensor", split_axis=0, concat_axis=0, tiled=True)
    summed = jnp.sum(received.astype(jnp.float32), axis=0)
    grad_own = (residual.astype(jnp.float32) + summed).astype(jnp.bfloat16)
    grad_rows = lax.all_gather(grad_own, "tensor", axis=0, tiled=True)
    contract_cols = (((1,), (1,)), ((), ()))
    hidden_grad = lax.dot_general(
        grad_rows, down_whole, contract_cols, preferred_element_type=jnp.float32
    )
    grad_up = (hidden_grad * gate * sig).astype(jnp.bfloat16)
    grad_gate = (hidden_grad * upper * sig * (1.0 + gate * (1.0 - sig))).astype(jnp.bfloat16)
    local_grad = lax.dot_general(
        teacher, grad_rows, (((0,), (0,)), ((), ())), preferred_element_type=jnp.float32
    )
    projector_grad = lax.psum_scatter(
        local_grad, "dp", scatter_dimension=1, tiled=True
    ) / math.sqrt(token_total)
    return (projector_grad, grad_own, grad_gate, grad_up)


def solution(mesh):
    in_specs = (
        P("dp", "tensor"),
        P("tensor", "dp"),
        P(("dp", "tensor"), None),
        P("dp", "tensor"),
        P("dp", "tensor"),
        P("tensor", "dp"),
    )
    out_specs = (P("tensor", "dp"), P(("dp", "tensor"), None), P("dp", "tensor"), P("dp", "tensor"))
    return jax.shard_map(
        per_device, mesh=mesh, in_specs=in_specs, out_specs=out_specs, check_vma=False
    )
```

profile of v0, /device:TPU:2, one launch (start us, length us, event | category | flops | bytes accessed | tf_op | source)
XLA Modules:
  0.0 417.5 jit_solution(8088165536229022003)
XLA Ops:
  7.2 0.0 copy-start
  7.2 0.0 all-gather.4.cloned.1.call-start
  7.2 0.7 all-gather.4.cloned.1.call-update
  7.9 0.0 all-gather.6.cloned.1.call-start
  8.0 0.7 all-gather.6.cloned.1.call-update
  8.7 0.0 all-gather.8.cloned.1.call-start
  8.7 95.7 %all-gather.4.cloned.1.call-done = bf16[1024,2048]{0,1:T(8,128)(2,1)} async-done(((bf16[1024,32]{0,1:T(8,128)(2,1)}), bf16[1024,2048]{0,1:T(8,128)(2,1)}) %all-gather.4.cloned.1.call-update) | async-done | bytes 4194320 | tf_op jit(solution)/shard_map/all_gather | solution.py:22
  104.4 3.9 fusion.11
  108.3 79.0 %all-gather.6.cloned.1.call-done = bf16[384,2048]{0,1:T(8,128)(2,1)} async-done(((bf16[384,32]{0,1:T(8,128)(2,1)}), bf16[384,2048]{0,1:T(8,128)(2,1)}) %all-gather.6.cloned.1.call-update) | async-done | bytes 1572880 | tf_op jit(solution)/shard_map/all_gather | solution.py:19
  187.4 0.0 copy-done
  187.4 2.1 fusion
  189.5 0.0 copy-start.2
  189.5 19.2 %all_to_all.5 = bf16[8,32,2048]{2,1,0:T(8,128)(2,1)S(1)} all-to-all(bf16[8,32,2048]{2,1,0:T(8,128)(2,1)S(1)} %bitcast.10), channel_id=1, replica_groups=mesh['dp'=64,'tensor'=8] {'tensor'}, dimensions={0} | all-to-all | bytes 2097152 | tf_op jit(solution)/shard_map/all_to_all | solution.py:26
  208.7 0.1 convert_reduce_fusion
  208.9 0.0 copy-done.2
  208.9 0.7 add_convert_fusion
  209.6 0.0 all-gather.8.cloned.1.call-update
  209.6 0.0 reduce-scatter.2.cloned.1.call-start
  209.6 40.8 %all-gather.8.cloned.1.call-done = bf16[256,2048]{1,0:T(8,128)(2,1)} async-done(((bf16[32,2048]{1,0:T(8,128)(2,1)}), bf16[256,2048]{1,0:T(8,128)(2,1)}) %all-gather.8.cloned.1.call-update) | async-done | bytes 1048592 | tf_op jit(solution)/shard_map/all_gather | solution.py:29
  250.4 3.7 convolution_bitcast_fusion
  254.1 0.0 copy-start.1
  254.1 0.0 copy-start.3
  254.1 0.0 copy-start.4
  254.1 0.0 reduce-scatter.2.cloned.1.call-update
  254.1 1.2 copy-done.1
  255.3 0.1 copy-done.3
  255.4 0.2 copy-done.4
  255.6 4.7 %fusion.10 = (bf16[256,1024]{1,0:T(8,128)(2,1)}, bf16[256,1024]{1,0:T(8,128)(2,1)}) fusion(bf16[256,1024]{1,0:T(8,128)(2,1)S(1)} %copy-done.4, bf16[256,1024]{1,0:T(8,128)(2,1)S(1)} %copy-done.3, bf16[256,2048]{1,0:T(8,128)(2,1)S(1)} %copy-done.1, bf16[1024,2048]{0,1:T(8,128)(2,1)} %all-gather.4.cloned.1.call-done), kind=kOutput, calls=%fused_computation.19 | convolution fusion | flops 1077673984 | bytes 7340032 | tf_op jit(solution)/shard_map/dot_general | solution.py:31
  260.3 149.3 %reduce-scatter.2.cloned.1.call-done = f32[384,32]{0,1:T(8,128)} async-done(((f32[384,2048]{0,1:T(8,128)}), f32[384,32]{0,1:T(8,128)}) %reduce-scatter.2.cloned.1.call-update) | async-done | bytes 49168 | tf_op jit(solution)/shard_map/reduce_scatter | solution.py:39
  409.6 1.4 broadcast_multiply_fusion
Async XLA Ops:
  7.2 180.2 %copy-start = (bf16[256,384]{1,0:T(8,128)(2,1)S(1)}, bf16[256,384]{1,0:T(8,128)(2,1)}, u32[]{:S(2)}) copy-start(bf16[256,384]{1,0:T(8,128)(2,1)} %param.6) | copy-start | bytes 589828
  7.2 97.2 %all-gather.4.cloned.1.call-start = ((), (), s32[]{:S(2)}) async-start(), calls=%async_computation.2 | async-start | bytes 4259840 | tf_op jit(solution)/shard_map/all_gather | solution.py:22
  7.9 179.4 %all-gather.6.cloned.1.call-start = ((), (), s32[]{:S(2)}) async-start(), calls=%async_computation.3 | async-start | bytes 1597440 | tf_op jit(solution)/shard_map/all_gather | solution.py:19
  8.7 241.8 %all-gather.8.cloned.1.call-start = ((), (), s32[]{:S(2)}) async-start(), calls=%async_computation.4 | async-start | bytes 1179648 | tf_op jit(solution)/shard_map/all_gather | solution.py:29
  189.5 19.4 %copy-start.2 = (bf16[32,2048]{1,0:T(8,128)(2,1)S(1)}, bf16[32,2048]{1,0:T(8,128)(2,1)}, u32[]{:S(2)}) copy-start(bf16[32,2048]{1,0:T(8,128)(2,1)} %param.8) | copy-start | bytes 393220
  209.6 200.0 %reduce-scatter.2.cloned.1.call-start = ((), (), s32[]{:S(2)}) async-start(), calls=%async_computation.5 | async-start | bytes 3194880 | tf_op jit(solution)/shard_map/reduce_scatter | solution.py:39
  254.1 1.2 copy-start.1
  254.1 1.4 copy-start.3
  254.1 1.5 copy-start.4
Sparse Core Ops, SparseCore 0:
  11.4 92.9 all-gather.3
  107.7 79.6 all-gather.5
  209.7 40.6 all-gather.7
  255.0 154.5 reduce-scatter.1
where the time goes:
time: 418 us
  waiting for transfers between devices  366 us (88%)
  blocking collectives  19.2 us (5%)
  matrix products  14.4 us (3%)
  between operations  13.8 us (3%)
    reduce_scatter x1, waiting for transfers between devices, per_device(): lax.psum_scatter(local_grad, 'dp', scatter_dimension=1, tiled=True)  149 us
    all_gather x1, waiting for transfers between devices, per_device(): down_whole = lax.all_gather(down_weight, 'dp', axis=1, tiled=True)  95.7 us
    all_gather x1, waiting for transfers between devices, per_device(): lax.all_gather(projector, 'dp', axis=1, tiled=True)  79 us
    all_gather x1, waiting for transfers between devices, per_device(): grad_rows = lax.all_gather(grad_own, 'tensor', axis=0, tiled=True)  40.8 us
    all_to_all x1, blocking collectives, per_device(): lax.all_to_all(stacked, 'tensor', split_axis=0, concat_axis=0, tiled=True)  19.2 us
  transfers between devices with their start and end apart: 4, of which 4 were waited for; matrix products, arithmetic and copies ran while one was open for 2% of the time, Pallas kernels for 0%

commit v1 on v0

--- a/solution.py
+++ b/solution.py
@@ -26,7 +26,8 @@
     received = lax.all_to_all(stacked, "tensor", split_axis=0, concat_axis=0, tiled=True)
     summed = jnp.sum(received.astype(jnp.float32), axis=0)
     grad_own = (residual.astype(jnp.float32) + summed).astype(jnp.bfloat16)
-    grad_rows = lax.all_gather(grad_own, "tensor", axis=0, tiled=True)
+    sent = jnp.stack([grad_own] * lax.axis_size("tensor"))
+    grad_rows = jnp.concatenate(lax.all_to_all(sent, "tensor", 0, 0), axis=0)
     contract_cols = (((1,), (1,)), ((), ()))
     hidden_grad = lax.dot_general(
         grad_rows, down_whole, contract_cols, preferred_element_type=jnp.float32

time: 418 us -> 389 us (0.931)
  the two profiles are of different devices: /device:TPU:2 before, /device:TPU:4 now
where the time goes in v1:
time: 389 us; the launch traced here: 388 us
  waiting for transfers between devices  322 us (83%)
  blocking collectives  36.4 us (9%)
  between operations  13.8 us (4%)
  matrix products  13.2 us (3%)
    reduce_scatter x1, waiting for transfers between devices, per_device(): lax.psum_scatter(local_grad, 'dp', scatter_dimension=1, tiled=True)  146 us
    all_gather x1, waiting for transfers between devices, per_device(): down_whole = lax.all_gather(down_weight, 'dp', axis=1, tiled=True)  95.7 us
    all_gather x1, waiting for transfers between devices, per_device(): lax.all_gather(projector, 'dp', axis=1, tiled=True)  79 us
    all_to_all x1, blocking collectives, per_device(): lax.all_to_all(stacked, 'tensor', split_axis=0, concat_axis=0, tiled=True)  18.6 us
    all_to_all x1, blocking collectives, per_device(): grad_rows = jnp.concatenate(lax.all_to_all(sent, 'tensor', 0, 0), axis=0)  17.8 us
  transfers between devices with their start and end apart: 3, of which 3 were waited for; matrix products, arithmetic and copies ran while one was open for 2% of the time, Pallas kernels for 0%

profile of v1, /device:TPU:4, one launch (start us, length us, event | category | flops | bytes accessed | tf_op | source)
XLA Modules:
  0.0 388.2 jit_solution(17288825465285491321)
XLA Ops:
  7.2 0.0 copy-start
  7.2 0.0 all-gather.3.cloned.1.call-start
  7.2 0.7 all-gather.3.cloned.1.call-update
  7.9 0.0 all-gather.5.cloned.1.call-start
  8.0 0.7 all-gather.5.cloned.1.call-update
  8.7 0.0 reduce-scatter.2.cloned.1.call-start
  8.7 95.7 %all-gather.3.cloned.1.call-done = bf16[1024,2048]{0,1:T(8,128)(2,1)} async-done(((bf16[1024,32]{0,1:T(8,128)(2,1)}), bf16[1024,2048]{0,1:T(8,128)(2,1)}) %all-gather.3.cloned.1.call-update) | async-done | bytes 4194320 | tf_op jit(solution)/shard_map/all_gather | solution.py:22
  104.4 3.9 %fusion.11 = f32[256,2048]{1,0:T(8,128)S(1)} fusion(bf16[1024,2048]{0,1:T(8,128)(2,1)} %all-gather.3.cloned.1.call-done, bf16[256,1024]{1,0:T(8,128)(2,1)} %param.10, bf16[256,1024]{1,0:T(8,128)(2,1)} %param.9), kind=kOutput, calls=%fused_computation.20 | convolution fusion | flops 1075838976 | bytes 7340032 | tf_op jit(solution)/shard_map/dot_general | solution.py:23
  108.3 79.0 %all-gather.5.cloned.1.call-done = bf16[384,2048]{0,1:T(8,128)(2,1)} async-done(((bf16[384,32]{0,1:T(8,128)(2,1)}), bf16[384,2048]{0,1:T(8,128)(2,1)}) %all-gather.5.cloned.1.call-update) | async-done | bytes 1572880 | tf_op jit(solution)/shard_map/all_gather | solution.py:19
  187.3 0.0 copy-done
  187.3 2.1 fusion
  189.5 0.0 copy-start.2
  189.5 18.6 %all_to_all.10 = bf16[8,32,2048]{2,1,0:T(8,128)(2,1)S(1)} all-to-all(bf16[8,32,2048]{2,1,0:T(8,128)(2,1)S(1)} %bitcast.13), channel_id=1, replica_groups=mesh['dp'=64,'tensor'=8] {'tensor'}, dimensions={0} | all-to-all | bytes 2097152 | tf_op jit(solution)/shard_map/all_to_all | solution.py:26
  208.1 0.1 convert_reduce_fusion
  208.2 0.0 copy-done.2
  208.3 0.0 copy-start.1
  208.3 0.1 stack.2
  208.4 17.8 %all_to_all.11 = bf16[8,32,2048]{2,1,0:T(8,128)(2,1)S(1)} all-to-all(bf16[8,32,2048]{2,1,0:T(8,128)(2,1)S(1)} %stack.2), channel_id=1, replica_groups=mesh['dp'=64,'tensor'=8] {'tensor'}, dimensions={0} | all-to-all | bytes 2097152 | tf_op jit(solution)/shard_map/all_to_all | solution.py:30
  226.2 2.4 convolution_bitcast_fusion
  228.6 0.0 copy-done.1
  228.6 0.0 copy-start.3
  228.6 0.0 copy-start.4
  228.6 0.0 reduce-scatter.2.cloned.1.call-update
  228.6 1.0 copy-done.3
  229.7 0.2 copy-done.4
  229.8 4.7 %fusion.10 = (bf16[256,1024]{1,0:T(8,128)(2,1)}, bf16[256,1024]{1,0:T(8,128)(2,1)}) fusion(bf16[256,1024]{1,0:T(8,128)(2,1)S(1)} %copy-done.4, bf16[256,1024]{1,0:T(8,128)(2,1)S(1)} %copy-done.3, bf16[256,2048]{1,0:T(8,128)(2,1)S(1)} %bitcast.12, bf16[1024,2048]{0,1:T(8,128)(2,1)} %all-gather.3.cloned.1.call-done), kind=kOutput, calls=%fused_computation.19 | convolution fusion | flops 1077673984 | bytes 7340032 | tf_op jit(solution)/shard_map/dot_general | solution.py:32
  234.5 145.8 %reduce-scatter.2.cloned.1.call-done = f32[384,32]{0,1:T(8,128)} async-done(((f32[384,2048]{0,1:T(8,128)}), f32[384,32]{0,1:T(8,128)}) %reduce-scatter.2.cloned.1.call-update) | async-done | bytes 49168 | tf_op jit(solution)/shard_map/reduce_scatter | solution.py:40
  380.3 1.4 broadcast_multiply_fusion
  (1 shorter events, 0.0 us)
Async XLA Ops:
  7.2 180.2 %copy-start = (bf16[256,384]{1,0:T(8,128)(2,1)S(1)}, bf16[256,384]{1,0:T(8,128)(2,1)}, u32[]{:S(2)}) copy-start(bf16[256,384]{1,0:T(8,128)(2,1)} %param.6) | copy-start | bytes 589828
  7.2 97.2 %all-gather.3.cloned.1.call-start = ((), (), s32[]{:S(2)}) async-start(), calls=%async_computation.3 | async-start | bytes 4259840 | tf_op jit(solution)/shard_map/all_gather | solution.py:22
  7.9 179.4 %all-gather.5.cloned.1.call-start = ((), (), s32[]{:S(2)}) async-start(), calls=%async_computation.4 | async-start | bytes 1597440 | tf_op jit(solution)/shard_map/all_gather | solution.py:19
  8.7 371.6 %reduce-scatter.2.cloned.1.call-start = ((), (), s32[]{:S(2)}) async-start(), calls=%async_computation.5 | async-start | bytes 3194880 | tf_op jit(solution)/shard_map/reduce_scatter | solution.py:40
  189.5 18.7 %copy-start.2 = (bf16[32,2048]{1,0:T(8,128)(2,1)S(1)}, bf16[32,2048]{1,0:T(8,128)(2,1)}, u32[]{:S(2)}) copy-start(bf16[32,2048]{1,0:T(8,128)(2,1)} %param.8) | copy-start | bytes 393220
  208.3 20.4 %copy-start.1 = (bf16[32,2048]{1,0:T(8,128)(2,1)}, bf16[32,2048]{1,0:T(8,128)(2,1)S(1)}, u32[]{:S(2)}) copy-start(bf16[32,2048]{1,0:T(8,128)(2,1)S(1)} %add_convert_fusion) | copy-start | bytes 393220
  228.6 1.0 copy-start.3
  228.6 1.2 copy-start.4
Sparse Core Ops, SparseCore 0:
  11.4 92.9 all-gather.2
  107.7 79.6 all-gather.4
  228.8 151.4 reduce-scatter.1
